TPU v7x, 512 devices: a whole 4x4x16 slice. The times are simulated.
512 devices in a mesh: chan: 16 (over z), tm: 32 (over y, x, core).
Axes of the slice: x: 4, y: 4, z: 16, core: 2. Of those that a mesh axis runs over, the one named last changes fastest.
Arguments:
- traces: bfloat16 [64, 1920, 2048], P('tm', None, 'chan'), may hold values from -6 to 6
- band_bins: int32 [512], replicated, may hold values from 1 to 959, as said below
- partners: int32 [16, 4], P('chan'), may hold values from 0 to 15, as said below
- partner_counts: int32 [16], P('chan'), may hold values from 1 to 4, as said below
Outputs:
- cross_spectra: bfloat16 [16, 4, 512, 2, 128, 128], P('chan', None, 'tm')
Inputs may be any that keep to these rules, and one draw needn't show every extreme that they name: `band_bins`: 512 distinct bin numbers in no particular order. `partners`: row b lists b itself first, then the other blocks whose pair with b is listed at b, each of them b + 1, b - 1 or b + 2. A pair of blocks one apart is listed at one of the two, a pair two apart at the lower one, so every pair of blocks at most two apart is listed exactly once. Slots from partner_counts[b] on hold b. `partner_counts`: the number of listed partners of block b, b itself included.
All inputs are finite; a program needn't handle non-finite values.
Results may differ from a plain program's by a relative error of at most 0.0063.
Values may be sent and summed in bfloat16 or wider, within the bound.
A program may use at most 64 MiB of HBM per device.

v0:
```python
import math

import jax
import jax.numpy as jnp
from jax import lax
from jax.sharding import PartitionSpec as P


def from_behind(value, axis, by):
    count = lax.axis_size(axis)
    pairs = [(i, i + by) for i in range(count) if 0 <= i + by < count]
    return lax.ppermute(value, axis, pairs)


def band_table(band_bins, samples):
    band_count = band_bins.shape[0]
    sample_index = jnp.arange(samples, dtype=jnp.int32)
    phase_index = band_bins[:, None] * sample_index[None, :] % samples
    angles = phase_index.astype(jnp.float32) * (2.0 * math.pi / samples)
    stacked = jnp.stack([jnp.cos(angles), -jnp.sin(angles)], axis=1)
    return stacked.reshape(2 * band_count, samples).astype(jnp.bfloat16)


def body(traces, band_bins, partners, partner_counts):
    transform_table = band_table(band_bins, traces.shape[1])
    spectra = jnp.einsum("ks,wsc->wkc", transform_table, traces, preferred_element_type=jnp.float32)
    band_power = jnp.mean(spectra * spectra, axis=1, keepdims=True)
    whitened = (spectra * lax.rsqrt(band_power + 1e-06)).astype(jnp.bfloat16)
    regrouped = lax.all_to_all(whitened, "tm", split_axis=1, concat_axis=0, tiled=True)
    window_count, bin_rows, channel_count = regrouped.shape
    local_block = regrouped.reshape(window_count, bin_rows // 2, 2, channel_count)
    block_number = lax.axis_index("chan")
    nearby = [local_block]
    for offset in (1, -1, 2):
        nearby.append(from_behind(local_block, "chan", -offset))
    stacked = jnp.stack(nearby)

    def fetch_block(partner):
        offset = partner - block_number
        near_index = (
            (offset == 1).astype(jnp.int32)
            + 2 * (offset == -1).astype(jnp.int32)
            + 3 * (offset == 2).astype(jnp.int32)
        )
        return lax.dynamic_index_in_dim(stacked, near_index, 0, keepdims=False)

    slot_total = partner_counts[0]

    def compute(partner):
        partner_block = fetch_block(partner)
        swapped = jnp.stack([-partner_block[:, :, 1], partner_block[:, :, 0]], axis=2)
        real_part = jnp.einsum(
            "wkpc,wkpd->kcd", local_block, partner_block, preferred_element_type=jnp.float32
        )
        imag_part = jnp.einsum(
            "wkpc,wkpd->kcd", local_block, swapped, preferred_element_type=jnp.float32
        )
        return jnp.stack([real_part, imag_part], axis=1).astype(jnp.bfloat16)

    def nothing(partner):
        return jnp.zeros((bin_rows // 2, 2, channel_count, channel_count), jnp.bfloat16)

    slot_rows = []
    for slot_index in range(partners.shape[1]):
        slot_rows.append(
            lax.cond(slot_index < slot_total, compute, nothing, partners[0, slot_index])
        )
    return jnp.stack(slot_rows)[None]


def solution(mesh):
    placed = (P("tm", None, "chan"), P(), P("chan", None), P("chan"))
    return jax.shard_map(
        body,
        mesh=mesh,
        in_specs=placed,
        out_specs=P("chan", None, "tm", None, None, None),
        check_vma=False,
    )
```

profile of v0, /device:TPU:352, one launch (start us, length us, event | category | flops | bytes accessed | tf_op | source)
XLA Modules:
  0.0 119.0 jit_solution(17584053600149057028)
XLA Ops:
  0.0 17.7 %cosine_convert_fusion = (bf16[512,1,1920]{2,0,1:T(8,128)(2,1)S(1)}, bf16[512,1,1920]{2,0,1:T(8,128)(2,1)S(1)}) fusion(s32[512]{0:T(512)} %param.13), kind=kLoop, calls=%fused_computation.58 | loop fusion | flops 11796480 | bytes 3934208 | tf_op jit(solution)/shard_map/convert.28
  17.7 0.4 pad_maximum_fusion.4
  18.1 6.0 %copy.25 = bf16[512,2,1920]{2,1,0:T(2,128)(2,1)} copy(bf16[512,2,1920]{2,0,1:T(8,128)(2,1)S(1)} %pad_maximum_fusion.4) | data formatting | bytes 7864320 | tf_op jit(solution)/shard_map/stack | solution.py:20
  24.1 9.0 %reshape.219 = bf16[1024,1920,1]{1,0,2:T(8,128)(2,1)} reshape(bf16[512,2,1920]{2,1,0:T(2,128)(2,1)} %copy.25) | data formatting | bytes 7864320 | tf_op jit(solution)/shard_map/convert_element_type | solution.py:21
  33.1 3.4 %multiply_reduce_fusion = (f32[2,128]{1,0:T(2,128)S(1)}, f32[1024,2,128]{2,0,1:T(8,128)S(1)}) fusion(bf16[1024,1920,1]{1,0,2:T(8,128)(2,1)} %reshape.219, bf16[2,1920,128]{2,1,0:T(8,128)(2,1)S(1)} %copy-done), kind=kOutput, calls=%fused_computation.65 | convolution fusion | flops 1007156992 | bytes 5964800 | tf_op jit(solution)/shard_map/ks,wsc->wkc/dot_general | solution.py:26
  36.5 0.1 fusion.37
  36.6 0.0 copy-start.1
  36.6 0.5 copy.26
  37.2 18.9 %all_to_all.15 = bf16[2,1024,128]{2,0,1:T(2,128)(2,1)S(1)} all-to-all(bf16[2,1024,128]{2,0,1:T(2,128)(2,1)S(1)} %copy.26), channel_id=1, replica_groups=mesh['chan'=16,'tm'=32] {'tm'}, dimensions={1} | all-to-all | bytes 1048576 | tf_op jit(solution)/shard_map/all_to_all | solution.py:29
  56.1 0.5 copy.27
  56.6 3.4 %collective-permute-start.2 = (bf16[64,16,2,128]{3,0,2,1:T(8,128)(2,1)S(1)}, bf16[64,16,2,128]{3,0,2,1:T(8,128)(2,1)S(1)}, u32[]{:S(2)}, u32[]{:S(2)}) collective-permute-start(bf16[64,16,2,128]{3,0,2,1:T(8,128)(2,1)S(1)} %bitcast.131), channel_id=1, source_target_pairs={{64,0},{96,32},{128,64},{160,96},{192,128},{224,160},{256,192},{28... | collective-permute-start | bytes 1572872 | tf_op jit(solution)/shard_map/ppermute | solution.py:12
  60.0 4.1 %collective-permute-start.1 = (bf16[64,16,2,128]{3,0,2,1:T(8,128)(2,1)S(1)}, bf16[64,16,2,128]{3,0,2,1:T(8,128)(2,1)S(1)}, u32[]{:S(2)}, u32[]{:S(2)}) collective-permute-start(bf16[64,16,2,128]{3,0,2,1:T(8,128)(2,1)S(1)} %bitcast.132), channel_id=1, source_target_pairs={{0,32},{32,64},{64,96},{96,128},{128,160},{160,192},{192,224},{224... | collective-permute-start | bytes 1572872 | tf_op jit(solution)/shard_map/ppermute | solution.py:12
  64.1 1.9 %collective-permute-start = (bf16[64,16,2,128]{3,0,2,1:T(8,128)(2,1)S(1)}, bf16[64,16,2,128]{3,0,2,1:T(8,128)(2,1)S(1)}, u32[]{:S(2)}, u32[]{:S(2)}) collective-permute-start(bf16[64,16,2,128]{3,0,2,1:T(8,128)(2,1)S(1)} %bitcast.133), channel_id=1, source_target_pairs={{32,0},{64,32},{96,64},{128,96},{160,128},{192,160},{224,192},{256... | collective-permute-start | bytes 1572872 | tf_op jit(solution)/shard_map/ppermute | solution.py:12
  66.7 19.4 %collective-permute-done.2 = bf16[64,16,2,128]{3,0,2,1:T(8,128)(2,1)S(1)} collective-permute-done((bf16[64,16,2,128]{3,0,2,1:T(8,128)(2,1)S(1)}, bf16[64,16,2,128]{3,0,2,1:T(8,128)(2,1)S(1)}, u32[]{:S(2)}, u32[]{:S(2)}) %collective-permute-start.2) | collective-permute-done | bytes 524320 | tf_op jit(solution)/shard_map/ppermute | solution.py:12
  86.1 10.4 %collective-permute-done = bf16[64,16,2,128]{3,0,2,1:T(8,128)(2,1)S(1)} collective-permute-done((bf16[64,16,2,128]{3,0,2,1:T(8,128)(2,1)S(1)}, bf16[64,16,2,128]{3,0,2,1:T(8,128)(2,1)S(1)}, u32[]{:S(2)}, u32[]{:S(2)}) %collective-permute-start) | collective-permute-done | bytes 524320 | tf_op jit(solution)/shard_map/ppermute | solution.py:12
  96.5 1.6 %pad_maximum_fusion.5 = bf16[4,64,16,2,128]{4,1,3,2,0:T(8,128)(2,1)} fusion(bf16[1,64,16,2,128]{4,1,3,2,0:T(8,128)(2,1)S(1)} %bitcast.140, bf16[1,64,16,2,128]{4,1,3,2,0:T(8,128)(2,1)S(1)} %bitcast.141, bf16[1,64,16,2,128]{4,1,3,2,0:T(8,128)(2,1)S(1)} %bitcast.142, bf16[1,64,16,2,128]{4,1,3,2,0:T(8,128)(2,1)S(1)} %bitcast.134), kind=kLoop, calls=%fused_computation.63 | loop fusion | flops 3145728 | bytes 4194304 | tf_op jit(solution)/shard_map/stack | solution.py:36
  98.1 4.7 %conditional.7 = (bf16[1,16,2,128,128]{4,3,2,1,0:T(8,128)(2,1)}) conditional(s32[]{:T(128)} %bitcast.52, () %tuple.41, (s32[1,4]{1,0:T(1,128)S(1)}, s32[]{:T(128)}, bf16[4,64,16,2,128]{4,1,3,2,0:T(8,128)(2,1)}, bf16[64,16,2,128]{3,0,2,1:T(8,128)(2,1)S(1)}) %tuple.68), branch_computations={%region_7.8_spmd, %region_8.9_spmd} | conditional | flops 135659536 | bytes 9437332 | solution.py:66
  98.1 0.7 slice.37
  99.5 1.1 dynamic-slice_bitcast_fusion.3
  100.6 0.4 fusion.27
  100.9 0.1 slice_negate_fusion.3
  101.0 0.4 fusion.26
  101.3 0.1 pad_maximum_fusion.3
  101.4 1.3 %copy.48 = bf16[1,16,2,128,128]{4,3,2,1,0:T(8,128)(2,1)} copy(bf16[1,16,2,128,128]{3,4,1,2,0:T(8,128)(2,1)S(1)} %pad_maximum_fusion.3) | data formatting | bytes 2097152 | tf_op jit(solution)/shard_map/cond | solution.py:66
  102.8 4.7 %conditional.6 = (bf16[1,16,2,128,128]{4,3,2,1,0:T(8,128)(2,1)}) conditional(s32[]{:T(128)} %bitcast.51, () %tuple.40, (s32[1,4]{1,0:T(1,128)S(1)}, s32[]{:T(128)}, bf16[4,64,16,2,128]{4,1,3,2,0:T(8,128)(2,1)}, bf16[64,16,2,128]{3,0,2,1:T(8,128)(2,1)S(1)}) %tuple.69), branch_computations={%region_5.6_spmd, %region_6.7_spmd} | conditional | flops 135659536 | bytes 9437332 | solution.py:66
  102.8 0.7 slice.34
  104.1 1.1 dynamic-slice_bitcast_fusion.2
  105.2 0.4 fusion.19
  105.6 0.1 slice_negate_fusion.2
  105.6 0.4 fusion.18
  106.0 0.1 pad_maximum_fusion.2
  106.1 1.3 %copy.46 = bf16[1,16,2,128,128]{4,3,2,1,0:T(8,128)(2,1)} copy(bf16[1,16,2,128,128]{3,4,1,2,0:T(8,128)(2,1)S(1)} %pad_maximum_fusion.2) | data formatting | bytes 2097152 | tf_op jit(solution)/shard_map/cond | solution.py:66
  107.4 4.4 %conditional.5 = (bf16[1,16,2,128,128]{4,3,2,1,0:T(8,128)(2,1)}) conditional(s32[]{:T(128)} %bitcast.50, () %tuple.39, (s32[1,4]{1,0:T(1,128)S(1)}, s32[]{:T(128)}, bf16[4,64,16,2,128]{4,1,3,2,0:T(8,128)(2,1)}, bf16[64,16,2,128]{3,0,2,1:T(8,128)(2,1)S(1)}) %tuple.70), branch_computations={%region_3.4_spmd, %region_4.5_spmd} | conditional | flops 135659536 | bytes 9437332 | solution.py:66
  107.4 0.6 slice.31
  108.6 1.1 dynamic-slice_bitcast_fusion.1
  109.6 0.4 fusion.11
  110.0 0.1 slice_negate_fusion.1
  110.1 0.4 fusion.10
  110.4 0.1 pad_maximum_fusion.1
  110.5 1.3 %copy.44 = bf16[1,16,2,128,128]{4,3,2,1,0:T(8,128)(2,1)} copy(bf16[1,16,2,128,128]{3,4,1,2,0:T(8,128)(2,1)S(1)} %pad_maximum_fusion.1) | data formatting | bytes 2097152 | tf_op jit(solution)/shard_map/cond | solution.py:66
  111.9 3.3 %conditional.4 = (bf16[1,16,2,128,128]{4,3,2,1,0:T(8,128)(2,1)}) conditional(s32[]{:T(128)} %bitcast.40, () %tuple.37, (s32[1,4]{1,0:T(1,128)S(1)}, s32[]{:T(128)}, bf16[4,64,16,2,128]{4,1,3,2,0:T(8,128)(2,1)}, bf16[64,16,2,128]{3,0,2,1:T(8,128)(2,1)S(1)}) %tuple.71), branch_computations={%region_1.2_spmd, %region_2.3_spmd} | conditional | flops 135659536 | bytes 9437324 | solution.py:66
  111.9 1.1 dynamic-slice_bitcast_fusion
  113.0 0.4 fusion.3
  113.4 0.1 slice_negate_fusion
  113.4 0.4 fusion.2
  113.8 0.1 pad_maximum_fusion
  113.9 1.3 %copy.42 = bf16[1,16,2,128,128]{4,3,2,1,0:T(8,128)(2,1)} copy(bf16[1,16,2,128,128]{3,4,1,2,0:T(8,128)(2,1)S(1)} %pad_maximum_fusion) | data formatting | bytes 2097152 | tf_op jit(solution)/shard_map/cond | solution.py:66
  115.2 3.8 %maximum_bitcast_fusion = bf16[1,4,16,2,128,128]{5,4,3,2,1,0:T(8,128)(2,1)} fusion(bf16[1,16,2,128,128]{4,3,2,1,0:T(8,128)(2,1)} %get-tuple-element.80, bf16[1,16,2,128,128]{4,3,2,1,0:T(8,128)(2,1)} %get-tuple-element.79, bf16[1,16,2,128,128]{4,3,2,1,0:T(8,128)(2,1)} %get-tuple-element.78, bf16[1,16,2,128,128]{4,3,2,1,0:T(8,128)(2,1)} %get-tuple-element.77), kind=kLoop, calls=%fused_computation.53 | loop fusion | flops 6291456 | bytes 8388608 | tf_op jit(solution)/shard_map/broadcast_in_dim | solution.py:68
  (5 shorter events, 0.0 us)
Async XLA Ops:
  0.0 33.1 %copy-start = (bf16[2,1920,128]{2,1,0:T(8,128)(2,1)S(1)}, bf16[2,1920,128]{2,1,0:T(8,128)(2,1)}, u32[]{:S(2)}) copy-start(bf16[2,1920,128]{2,1,0:T(8,128)(2,1)} %param.12) | copy-start | bytes 2949124
  36.6 61.5 %copy-start.1 = (s32[1,4]{1,0:T(1,128)S(1)}, s32[1,4]{1,0:T(1,128)}, u32[]{:S(2)}) copy-start(s32[1,4]{1,0:T(1,128)} %param.14) | copy-start | bytes 52
  56.6 29.5 %collective-permute-start.2 = (bf16[64,16,2,128]{3,0,2,1:T(8,128)(2,1)S(1)}, bf16[64,16,2,128]{3,0,2,1:T(8,128)(2,1)S(1)}, u32[]{:S(2)}, u32[]{:S(2)}) collective-permute-start(bf16[64,16,2,128]{3,0,2,1:T(8,128)(2,1)S(1)} %bitcast.131), channel_id=1, source_target_pairs={{64,0},{96,32},{128,64},{160,96},{192,128},{224,160},{256,192},{28... | collective-permute-start | bytes 1572872 | tf_op jit(solution)/shard_map/ppermute | solution.py:12
  60.0 26.1 %collective-permute-start.1 = (bf16[64,16,2,128]{3,0,2,1:T(8,128)(2,1)S(1)}, bf16[64,16,2,128]{3,0,2,1:T(8,128)(2,1)S(1)}, u32[]{:S(2)}, u32[]{:S(2)}) collective-permute-start(bf16[64,16,2,128]{3,0,2,1:T(8,128)(2,1)S(1)} %bitcast.132), channel_id=1, source_target_pairs={{0,32},{32,64},{64,96},{96,128},{128,160},{160,192},{192,224},{224... | collective-permute-start | bytes 1572872 | tf_op jit(solution)/shard_map/ppermute | solution.py:12
  64.1 32.4 %collective-permute-start = (bf16[64,16,2,128]{3,0,2,1:T(8,128)(2,1)S(1)}, bf16[64,16,2,128]{3,0,2,1:T(8,128)(2,1)S(1)}, u32[]{:S(2)}, u32[]{:S(2)}) collective-permute-start(bf16[64,16,2,128]{3,0,2,1:T(8,128)(2,1)S(1)} %bitcast.133), channel_id=1, source_target_pairs={{32,0},{64,32},{96,64},{128,96},{160,128},{192,160},{224,192},{256... | collective-permute-start | bytes 1572872 | tf_op jit(solution)/shard_map/ppermute | solution.py:12
where the time goes:
time: 120 us; the launch traced here: 119 us
  waiting for transfers between devices  29.8 us (25%)
  local copies, waits for them, and re-layouts  27.6 us (23%)
  other arithmetic  24.2 us (20%)
  blocking collectives  18.9 us (16%)
  starting transfers between devices  9.42 us (8%)
  matrix products  6.19 us (5%)
  loops' own time  2.17 us (2%)
    ppermute x3, waiting for transfers between devices, from_behind(): return lax.ppermute(value, axis, pairs)  29.8 us
    all_to_all x1, blocking collectives, body(): lax.all_to_all(whitened, 'tm', split_axis=1, concat_axis=0, tiled=True)  18.9 us
    another operation x1, other arithmetic  17.7 us
    ppermute x3, starting transfers between devices, from_behind(): return lax.ppermute(value, axis, pairs)  9.42 us
    convert_element_type x1, local copies, waits for them, and re-layouts, band_table(): return stacked.reshape(2 * band_count, samples).astype(jnp.bfloat16)  9.03 us
    another operation x1, local copies, waits for them, and re-layouts, band_table(): stacked = jnp.stack([jnp.cos(angles), -jnp.sin(angles)], axis=1)  5.97 us
    cond x4, local copies, waits for them, and re-layouts, body(): lax.cond(slot_index < slot_total, compute, nothing, partners[0, slot_index])  5.32 us
    squeeze x4, local copies, waits for them, and re-layouts, fetch_block(): return lax.dynamic_index_in_dim(stacked, near_index, 0, keepdims=False)  4.34 us
  transfers between devices with their start and end apart: 3, of which 2 were waited for; matrix products, arithmetic and copies ran while one was open for 0% of the time, Pallas kernels for 0%

commit v1 on v0

v1 whole, which is shorter than its diff:
```python
import functools
import math

import jax
import jax.numpy as jnp
from jax import lax
from jax.experimental import pallas as pl
from jax.experimental.pallas import tpu as pltpu
from jax.sharding import PartitionSpec as P

LANES = 128
MESH = pl.DeviceIdType.MESH


def unit_circle(turns_number, samples):
    quarter = samples // 4
    quadrant = jnp.floor(turns_number * (1.0 / quarter) + 0.5)
    x = (turns_number - quadrant * quarter) * (math.pi / 2 / quarter)
    y = x * x
    sine = x * (1 + y * (-1 / 6 + y * (1 / 120 + y * (-1 / 5040 + y * (1 / 362880)))))
    cosine = 1 + y * (-1 / 2 + y * (1 / 24 + y * (-1 / 720 + y * (1 / 40320 + y * (-1 / 3628800)))))
    which = quadrant.astype(jnp.int32)
    odd = (which & 1) == 1
    c = jnp.where(odd, sine, cosine)
    s = jnp.where(odd, cosine, sine)
    c = jnp.where(((which + 1) & 2) == 2, -c, c)
    s = jnp.where((which & 2) == 2, -s, s)
    return c, s


def spectra_kernel(bins_ref, traces_ref, send_ref, table_ref, spectra_ref):
    windows, samples, channels = traces_ref.shape
    groups, group = bins_ref.shape
    bin_count = groups * group
    lane = lax.broadcasted_iota(jnp.int32, (group, LANES), 1).astype(jnp.float32)
    both = jnp.concatenate([traces_ref[w] for w in range(windows)], axis=1)
    power = jnp.zeros((1, windows * channels), jnp.float32)
    for g in range(groups):
        row = bins_ref[g : g + 1, :].astype(jnp.float32)
        number = jnp.broadcast_to(row, (group, group)).T
        number = number[:, :LANES]
        c, s = unit_circle(number * lane, samples)
        step_c, step_s = unit_circle(number * float(LANES), samples)
        for q in range(samples // LANES):
            table_ref[g % 2, :group, q * LANES : (q + 1) * LANES] = c.astype(jnp.bfloat16)
            table_ref[g % 2, group:, q * LANES : (q + 1) * LANES] = (-s).astype(jnp.bfloat16)
            c, s = c * step_c - s * step_s, s * step_c + c * step_s
        y = jnp.dot(table_ref[g % 2], both, preferred_element_type=jnp.float32)
        spectra_ref[g] = y
        power = power + jnp.sum(y * y, axis=0, keepdims=True)
    scale = lax.rsqrt(power * (1.0 / (2 * bin_count)) + 1e-06)
    per = group // 16
    for g in range(groups):
        y = (spectra_ref[g] * scale).reshape(2, per, 2, 8, windows * channels)
        for h in range(2):
            parts = []
            for w in range(windows):
                for p in range(2):
                    parts.append(y[p, :, h, :, w * channels : (w + 1) * channels])
            send_ref[h, g * per : (g + 1) * per] = jnp.concatenate(parts, axis=1).astype(jnp.bfloat16)


def exchange_kernel(tm_count, send_ref, out_ref, held, wide, regrouped, local_sem, out_sem, in_sem,
                    down_send, down_recv, up_send, up_recv, relay_send, relay_recv):
    me = lax.axis_index("tm")
    block = lax.axis_index("chan")
    blocks = lax.axis_size("chan")
    has_below = block > 0
    has_above = block < blocks - 1
    pieces = down_send.shape[0]
    bins = regrouped.shape[0]
    size = bins // pieces
    rows = send_ref.shape[2]
    channels = send_ref.shape[3]
    windows = rows // 16 * tm_count

    barrier = pltpu.get_barrier_semaphore()

    @pl.loop(1, tm_count)
    def _(r):
        pl.semaphore_signal(barrier, inc=1, device_id=(block, lax.rem(me + r, tm_count)), device_id_type=MESH)

    @pl.when(has_below)
    def _():
        pl.semaphore_signal(barrier, inc=1, device_id=(block - 1, me), device_id_type=MESH)

    @pl.when(has_above)
    def _():
        pl.semaphore_signal(barrier, inc=1, device_id=(block + 1, me), device_id_type=MESH)

    others = has_below.astype(jnp.int32) + has_above.astype(jnp.int32)
    pl.semaphore_wait(barrier, tm_count - 1 + others)

    for h in range(2):
        @pl.loop(1, tm_count)
        def _(r):
            to = lax.rem(me + r, tm_count)
            pltpu.make_async_remote_copy(
                src_ref=send_ref.at[h, to], dst_ref=held.at[h, me],
                send_sem=out_sem.at[h], recv_sem=in_sem.at[h],
                device_id=(block, to), device_id_type=MESH).start()

        held[h, me] = send_ref[h, me]

    def down(q):
        part = pl.ds(q * size, size)
        return pltpu.make_async_remote_copy(
            src_ref=regrouped.at[part], dst_ref=out_ref.at[1, part],
            send_sem=down_send.at[q], recv_sem=down_recv.at[q],
            device_id=(block - 1, me), device_id_type=MESH)

    def up(q):
        part = pl.ds(q * size, size)
        return pltpu.make_async_remote_copy(
            src_ref=regrouped.at[part], dst_ref=out_ref.at[2, part],
            send_sem=up_send.at[q], recv_sem=up_recv.at[q],
            device_id=(block + 1, me), device_id_type=MESH)

    def relay(q):
        part = pl.ds(q * size, size)
        return pltpu.make_async_remote_copy(
            src_ref=out_ref.at[1, part], dst_ref=out_ref.at[3, part],
            send_sem=relay_send.at[q], recv_sem=relay_recv.at[q],
            device_id=(block - 1, me), device_id_type=MESH)

    def keep(q):
        part = pl.ds(q * size, size)
        return pltpu.make_async_copy(regrouped.at[part], out_ref.at[0, part], local_sem.at[q])

    for h in range(2):
        whole = held.at[h, pl.ds(0, tm_count - 1)]
        pltpu.make_async_copy(whole, whole, in_sem.at[h]).wait()
        wide[...] = held[h].astype(jnp.float32).reshape(tm_count * rows, channels)
        for q in range(h * pieces // 2, (h + 1) * pieces // 2):
            for j in range(size):
                at = q * size + j
                for p in range(2):
                    start = at - 8 * h + 8 * p
                    lines = wide[pl.ds(start, windows, stride=16), :]
                    regrouped[at, p * windows : (p + 1) * windows, :] = lines.astype(jnp.bfloat16)

            @pl.when(has_below)
            def _():
                down(q).start()

            @pl.when(has_above)
            def _():
                up(q).start()

            keep(q).start()

    for q in range(pieces):
        @pl.when(has_above)
        def _():
            down(q).wait_recv()

        @pl.when(has_above & has_below)
        def _():
            relay(q).start()

    for q in range(pieces):
        keep(q).wait()

        @pl.when(has_below)
        def _():
            up(q).wait_recv()
            down(q).wait_send()

        @pl.when(has_above)
        def _():
            up(q).wait_send()

        @pl.when(block < blocks - 2)
        def _():
            relay(q).wait_recv()

        @pl.when(has_above & has_below)
        def _():
            relay(q).wait_send()

    for h in range(2):
        whole = held.at[h, pl.ds(0, tm_count - 1)]
        pltpu.make_async_copy(whole, whole, out_sem.at[h]).wait()


def product_kernel(partners_ref, counts_ref, blocks_ref, out_ref):
    block = lax.axis_index("chan")
    bins, depth, channels = blocks_ref.shape[1:]
    half = depth // 2
    slots = out_ref.shape[1]
    where_from = []
    for slot in range(slots):
        offset = partners_ref[0, slot] - block
        where_from.append(jnp.where(offset == 1, 1, jnp.where(offset == -1, 2, jnp.where(offset == 2, 3, 0))))
    for k in range(bins):
        own = blocks_ref[0, k]
        turned = jnp.concatenate([own[half:], -own[:half]], axis=0)
        left = jnp.concatenate([own, turned], axis=1)
        for slot in range(slots):
            @pl.when(slot < counts_ref[0])
            def _():
                other = blocks_ref[where_from[slot], k]
                both = lax.dot_general(left, other, (((0,), (0,)), ((), ())), preferred_element_type=jnp.float32)
                out_ref[0, slot, k] = both.astype(jnp.bfloat16).reshape(2, channels, channels)

            @pl.when(slot >= counts_ref[0])
            def _():
                out_ref[0, slot, k] = jnp.zeros((2, channels, channels), jnp.bfloat16)


def body(traces, band_bins, partners, partner_counts):
    windows, samples, channels = traces.shape
    bin_count = band_bins.shape[0]
    tm_count = lax.axis_size("tm")
    group = min(128, bin_count)
    groups = bin_count // group
    bins = bin_count // tm_count
    rows = 16 * windows
    send = pl.pallas_call(
        spectra_kernel,
        out_shape=jax.ShapeDtypeStruct((2, tm_count, rows, channels), jnp.bfloat16),
        in_specs=[pl.BlockSpec(memory_space=pltpu.VMEM)] * 2,
        out_specs=pl.BlockSpec(memory_space=pltpu.VMEM),
        scratch_shapes=[
            pltpu.VMEM((2, 2 * group, samples), jnp.bfloat16),
            pltpu.VMEM((groups, 2 * group, windows * channels), jnp.float32),
        ],
        compiler_params=pltpu.CompilerParams(vmem_limit_bytes=48 << 20),
        name="spectra",
    )(band_bins.reshape(groups, group), traces)

    pieces = 4
    depth = 2 * windows * tm_count
    blocks = pl.pallas_call(
        functools.partial(exchange_kernel, tm_count),
        out_shape=jax.ShapeDtypeStruct((4, bins, depth, channels), jnp.bfloat16),
        in_specs=[pl.BlockSpec(memory_space=pltpu.VMEM)],
        out_specs=pl.BlockSpec(memory_space=pl.ANY),
        scratch_shapes=[
            pltpu.VMEM((2, tm_count, rows, channels), jnp.bfloat16),
            pltpu.VMEM((tm_count * rows, channels), jnp.float32),
            pltpu.VMEM((bins, depth, channels), jnp.bfloat16),
            pltpu.SemaphoreType.DMA((pieces,)),
            pltpu.SemaphoreType.DMA((2,)),
            pltpu.SemaphoreType.DMA((2,)),
        ] + [pltpu.SemaphoreType.DMA((pieces,))] * 6,
        compiler_params=pltpu.CompilerParams(
            collective_id=0, has_side_effects=True, vmem_limit_bytes=48 << 20),
        name="exchange",
    )(send)

    step = 4
    return pl.pallas_call(
        product_kernel,
        grid=(bins // step,),
        out_shape=jax.ShapeDtypeStruct((1, 4, bins, 2, channels, channels), jnp.bfloat16),
        in_specs=[
            pl.BlockSpec(memory_space=pltpu.SMEM),
            pl.BlockSpec(memory_space=pltpu.SMEM),
            pl.BlockSpec((4, step, depth, channels), lambda i: (0, i, 0, 0)),
        ],
        out_specs=pl.BlockSpec((1, 4, step, 2, channels, channels), lambda i: (0, 0, i, 0, 0, 0)),
        compiler_params=pltpu.CompilerParams(vmem_limit_bytes=48 << 20),
        name="products",
    )(partners, partner_counts, blocks)


def solution(mesh):
    placed = (P("tm", None, "chan"), P(), P("chan", None), P("chan"))
    return jax.shard_map(
        body,
        mesh=mesh,
        in_specs=placed,
        out_specs=P("chan", None, "tm", None, None, None),
        check_vma=False,
    )
```

time: 120 us -> 59.1 us (0.49)
  the two profiles are of different devices: /device:TPU:352 before, /device:TPU:33 now
where the time goes in v1:
time: 59.1 us; the launch traced here: 58.9 us
  Pallas kernels  55.7 us (94%)
  local copies, waits for them, and re-layouts  2.53 us (4%)
  between operations  0.69 us (1%)
    pallas_call x1, Pallas kernels, body(): pl.pallas_call(functools.partial(exchange_kernel, tm_count), out_shape=ja...  38.5 us
    pallas_call x1, Pallas kernels, body(): pl.pallas_call(product_kernel, grid=(bins // step,), out_shape=jax.ShapeD...  14.3 us
    pallas_call x1, Pallas kernels, body(): pl.pallas_call(spectra_kernel, out_shape=jax.ShapeDtypeStruct((2, tm_coun...  2.85 us
    unnamed x6, local copies, waits for them, and re-layouts  2.53 us

profile of v1, /device:TPU:33, one launch (start us, length us, event | category | flops | bytes accessed | tf_op | source)
XLA Modules:
  0.0 58.9 jit_solution(2146300895694365095)
XLA Ops:
  0.7 0.0 copy-start
  0.7 1.2 %copy-done = bf16[2,1920,128]{2,1,0:T(8,128)(2,1)S(1)} copy-done((bf16[2,1920,128]{2,1,0:T(8,128)(2,1)S(1)}, bf16[2,1920,128]{2,1,0:T(8,128)(2,1)}, u32[]{:S(2)}) %copy-start) | copy-done | bytes 983064
  1.9 0.0 copy-start.1
  1.9 0.7 %copy-done.1 = s32[512]{0:T(512)S(1)} copy-done((s32[512]{0:T(512)S(1)}, s32[512]{0:T(512)}, u32[]{:S(2)}) %copy-start.1) | copy-done | bytes 2072
  2.5 2.9 %spectra.1.send_ref = bf16[2,32,32,128]{3,2,1,0:T(8,128)(2,1)S(1)} custom-call(s32[4,128]{1,0:T(4,128)S(1)} %bitcast.1, bf16[2,1920,128]{2,1,0:T(8,128)(2,1)S(1)} %copy-done), custom_call_target="tpu_custom_call" | custom-call | tf_op jit(solution)/shard_map/spectra/pallas_call | solution.py:219
  5.4 38.5 %exchange.1.blocks_ref = bf16[4,16,128,128]{3,2,1,0:T(8,128)(2,1)S(1)} custom-call(bf16[2,32,32,128]{3,2,1,0:T(8,128)(2,1)S(1)} %spectra.1.send_ref), custom_call_target="tpu_custom_call" | custom-call | tf_op jit(solution)/shard_map/exchange/pallas_call | solution.py:234
  43.9 0.0 copy-start.2
  43.9 0.6 %copy-done.2 = s32[1,4]{1,0:T(1,128)S(1)} copy-done((s32[1,4]{1,0:T(1,128)S(1)}, s32[1,4]{1,0:T(1,128)}, u32[]{:S(2)}) %copy-start.2) | copy-done | bytes 40
  44.6 14.3 %products.1 = bf16[1,4,16,2,128,128]{5,4,3,2,1,0:T(8,128)(2,1)} custom-call(s32[1,4]{1,0:T(1,128)S(1)} %copy-done.2, s32[1]{0:T(128)S(6)} %copy.5.counts_ref, bf16[4,16,128,128]{3,2,1,0:T(8,128)(2,1)S(1)} %exchange.1.blocks_ref), custom_call_target="tpu_custom_call" | custom-call | tf_op jit(solution)/shard_map/products/pallas_call | solution.py:253
Async XLA Ops:
  0.7 1.2 %copy-start = (bf16[2,1920,128]{2,1,0:T(8,128)(2,1)S(1)}, bf16[2,1920,128]{2,1,0:T(8,128)(2,1)}, u32[]{:S(2)}) copy-start(bf16[2,1920,128]{2,1,0:T(8,128)(2,1)} %traces_ref.1) | copy-start | bytes 2949124
  1.9 0.7 %copy-start.1 = (s32[512]{0:T(512)S(1)}, s32[512]{0:T(512)}, u32[]{:S(2)}) copy-start(s32[512]{0:T(512)} %param.5) | copy-start | bytes 6148
  43.9 0.7 %copy-start.2 = (s32[1,4]{1,0:T(1,128)S(1)}, s32[1,4]{1,0:T(1,128)}, u32[]{:S(2)}) copy-start(s32[1,4]{1,0:T(1,128)} %partners_ref.1) | copy-start | bytes 52

commit v2 on v0

v2 whole, which is shorter than its diff:
```python
import functools
import math

import jax
import jax.numpy as jnp
from jax import lax
from jax.experimental import pallas as pl
from jax.experimental.pallas import tpu as pltpu
from jax.sharding import PartitionSpec as P

LANES = 128
MESH = pl.DeviceIdType.MESH


def unit_circle(turns_number, samples):
    quarter = samples // 4
    quadrant = jnp.floor(turns_number * (1.0 / quarter) + 0.5)
    x = (turns_number - quadrant * quarter) * (math.pi / 2 / quarter)
    y = x * x
    sine = x * (1 + y * (-1 / 6 + y * (1 / 120 + y * (-1 / 5040 + y * (1 / 362880)))))
    cosine = 1 + y * (-1 / 2 + y * (1 / 24 + y * (-1 / 720 + y * (1 / 40320 + y * (-1 / 3628800)))))
    which = quadrant.astype(jnp.int32)
    odd = (which & 1) == 1
    c = jnp.where(odd, sine, cosine)
    s = jnp.where(odd, cosine, sine)
    c = jnp.where(((which + 1) & 2) == 2, -c, c)
    s = jnp.where((which & 2) == 2, -s, s)
    return c, s


def exchange_kernel(tm_count, bins_hbm, traces_hbm, made_ref, left_ref, last_ref, bins_ref, traces_ref, table_ref, spectra_ref,
                    send_ref, held, upper, lower, second, wide, block_ref, load_sem, out_sem, in_sem,
                    down_send, down_recv, up_send, up_recv, relay_send, relay_recv):
    me = lax.axis_index("tm")
    block = lax.axis_index("chan")
    blocks = lax.axis_size("chan")
    has_below = block > 0
    has_above = block < blocks - 1
    windows, samples, channels = traces_ref.shape
    groups, group = bins_ref.shape
    bin_count = groups * group
    rows = send_ref.shape[1]
    chips = tm_count // 2
    side = math.isqrt(chips)
    chip = me // 2
    core = lax.rem(me, 2)
    chip_y = chip // side
    chip_x = lax.rem(chip, side)

    barrier = pltpu.get_barrier_semaphore()

    load_bins = pltpu.make_async_copy(bins_hbm, bins_ref, load_sem.at[0])
    load_traces = pltpu.make_async_copy(traces_hbm, traces_ref, load_sem.at[1])
    load_bins.start()
    load_traces.start()

    @pl.loop(1, tm_count)
    def _(r):
        pl.semaphore_signal(barrier, inc=1, device_id=(block, lax.rem(me + r, tm_count)), device_id_type=MESH)

    @pl.when(has_below)
    def _():
        pl.semaphore_signal(barrier, inc=1, device_id=(block - 1, me), device_id_type=MESH)

    @pl.when(has_above)
    def _():
        pl.semaphore_signal(barrier, inc=1, device_id=(block + 1, me), device_id_type=MESH)

    lane = lax.broadcasted_iota(jnp.int32, (group, LANES), 1).astype(jnp.float32)
    load_bins.wait()
    power = jnp.zeros((1, windows * channels), jnp.float32)
    for g in range(groups):
        row = bins_ref[g : g + 1, :].astype(jnp.float32)
        number = jnp.broadcast_to(row, (group, group)).T
        c, s = unit_circle(number * lane, samples)
        step_c, step_s = unit_circle(number * float(LANES), samples)
        for q in range(samples // LANES):
            table_ref[g % 2, :group, q * LANES : (q + 1) * LANES] = c.astype(jnp.bfloat16)
            table_ref[g % 2, group:, q * LANES : (q + 1) * LANES] = (-s).astype(jnp.bfloat16)
            c, s = c * step_c - s * step_s, s * step_c + c * step_s
        if g == 0:
            load_traces.wait()
        both = jnp.concatenate([traces_ref[w] for w in range(windows)], axis=1)
        y = jnp.dot(table_ref[g % 2], both, preferred_element_type=jnp.float32)
        spectra_ref[g] = y
        power = power + jnp.sum(y * y, axis=0, keepdims=True)
    scale = lax.rsqrt(power * (1.0 / (2 * bin_count)) + 1e-06)
    per = group // 16
    for g in range(groups):
        y = (spectra_ref[g] * scale).reshape(2, per, 2, 8, windows * channels)
        parts = []
        for w in range(windows):
            for h in range(2):
                for p in range(2):
                    parts.append(y[p, :, h, :, w * channels : (w + 1) * channels])
        send_ref[g * per : (g + 1) * per] = jnp.concatenate(parts, axis=1).astype(jnp.bfloat16)

    others = has_below.astype(jnp.int32) + has_above.astype(jnp.int32)
    pl.semaphore_wait(barrier, tm_count - 1 + others)

    def fold(d):
        return d + d // 2 - 2 * (d // 3)

    def chip_at(step, sign):
        dy, dx = fold(step // side), fold(lax.rem(step, side))
        return lax.rem(chip_y + sign * dy + side, side) * side + lax.rem(chip_x + sign * dx + side, side)

    def spread(to):
        pltpu.make_async_remote_copy(
            src_ref=send_ref.at[to], dst_ref=held.at[me],
            send_sem=out_sem, recv_sem=in_sem.at[chip],
            device_id=(block, to), device_id_type=MESH).start()

    def pair(ref, f):
        return ref.at[pl.ds(f * 2, 2)]

    def down(f):
        return pltpu.make_async_remote_copy(
            src_ref=pair(held, f), dst_ref=pair(upper, f), send_sem=down_send, recv_sem=down_recv.at[f],
            device_id=(block - 1, me), device_id_type=MESH)

    def up(f):
        return pltpu.make_async_remote_copy(
            src_ref=pair(held, f), dst_ref=pair(lower, f), send_sem=up_send, recv_sem=up_recv,
            device_id=(block + 1, me), device_id_type=MESH)

    def relay(f):
        return pltpu.make_async_remote_copy(
            src_ref=pair(upper, f), dst_ref=pair(second, f), send_sem=relay_send, recv_sem=relay_recv,
            device_id=(block - 1, me), device_id_type=MESH)

    def forward(f):
        @pl.when(has_below)
        def _():
            down(f).start()

        @pl.when(has_above)
        def _():
            up(f).start()

    def wait_for(ref, sem):
        pltpu.make_async_copy(ref, ref, sem).wait()

    spread(chip * 2 + 1 - core)

    @pl.loop(1, chips)
    def _(step):
        to = chip_at(step, 1)
        spread(to * 2 + core)
        spread(to * 2 + 1 - core)

    held[me] = send_ref[me]
    wait_for(held.at[0], in_sem.at[chip])
    forward(chip)

    @pl.loop(1, chips)
    def _(step):
        f = chip_at(step, -1)
        wait_for(pair(held, 0), in_sem.at[f])
        forward(f)

    total = tm_count * windows

    def regroup(ref, to_ref):
        wide[...] = ref[...].astype(jnp.float32).reshape(tm_count * rows, channels)
        for j in range(16):
            for p in range(2):
                lines = wide[pl.ds(j // 8 * 16 + p * 8 + j % 8, total, stride=32), :]
                to_ref[j, p * total : (p + 1) * total, :] = lines.astype(jnp.bfloat16)

    def products(where):
        @pl.loop(0, 16)
        def _(j):
            both = jnp.dot(left_ref[j], block_ref[j], preferred_element_type=jnp.float32)
            made_ref[where, j] = both.astype(jnp.bfloat16).reshape(2, channels, channels)

    @pl.when(has_above)
    def _():
        @pl.loop(0, chips)
        def _(step):
            f = chip_at(step, -1)
            wait_for(pair(upper, 0), down_recv.at[f])

            @pl.when(has_below)
            def _():
                relay(f).start()

    regroup(held, block_ref)

    @pl.loop(0, 16)
    def _(j):
        own = block_ref[j]
        left_ref[j, :channels, :] = own.T
        left_ref[j, channels:, :] = jnp.concatenate([own[total:], -own[:total]], axis=0).T

    products(0)

    @pl.when(has_above)
    def _():
        regroup(upper, block_ref)
        products(1)

    @pl.when(has_below)
    def _():
        wait_for(lower, up_recv)
        regroup(lower, block_ref)
        products(2)

    wait_for(held.at[pl.ds(0, tm_count - 1)], out_sem)

    @pl.when(has_below)
    def _():
        wait_for(held, down_send)

    @pl.when(has_above)
    def _():
        wait_for(held, up_send)

    @pl.when(has_above & has_below)
    def _():
        wait_for(held, relay_send)

    @pl.when(block < blocks - 2)
    def _():
        wait_for(second, relay_recv)
        regroup(second, last_ref)


def place_kernel(counts_ref, partners_hbm, made_ref, left_ref, last_ref, out_hbm,
                 partners_ref, product_ref, zero_ref, load_sem, out_sem):
    block = lax.axis_index("chan")
    bins, _, channels = last_ref.shape
    slots = out_hbm.shape[1]
    load_partners = pltpu.make_async_copy(partners_hbm, partners_ref, load_sem)
    load_partners.start()
    pltpu.make_async_copy(made_ref.at[0], out_hbm.at[0, 0], out_sem).start()
    zero_ref[...] = jnp.zeros_like(zero_ref)
    load_partners.wait()
    for slot in range(1, slots):
        offset = partners_ref[0, slot] - block
        listed = slot < counts_ref[0]

        @pl.when(listed & (offset == 1))
        def _():
            pltpu.make_async_copy(made_ref.at[1], out_hbm.at[0, slot], out_sem).start()

        @pl.when(listed & (offset == -1))
        def _():
            pltpu.make_async_copy(made_ref.at[2], out_hbm.at[0, slot], out_sem).start()

        @pl.when(jnp.logical_not(listed))
        def _():
            for k in range(0, bins, zero_ref.shape[0]):
                to = out_hbm.at[0, slot, pl.ds(k, zero_ref.shape[0])]
                pltpu.make_async_copy(zero_ref, to, out_sem).start()

    for slot in range(1, slots):
        @pl.when((slot < counts_ref[0]) & (partners_ref[0, slot] - block == 2))
        def _():
            for k in range(bins):
                both = jnp.dot(left_ref[k], last_ref[k], preferred_element_type=jnp.float32)
                product_ref[k] = both.astype(jnp.bfloat16).reshape(2, channels, channels)
                if k % 2 == 1:
                    part = pl.ds(k - 1, 2)
                    pltpu.make_async_copy(product_ref.at[part], out_hbm.at[0, slot, part], out_sem).start()

    for slot in range(slots):
        pltpu.make_async_copy(made_ref.at[0], out_hbm.at[0, slot], out_sem).wait()


def body(traces, band_bins, partners, partner_counts):
    windows, samples, channels = traces.shape
    bin_count = band_bins.shape[0]
    tm_count = lax.axis_size("tm")
    group = min(128, bin_count)
    groups = bin_count // group
    bins = bin_count // tm_count
    rows = 32 * windows
    chips = tm_count // 2
    depth = 2 * windows * tm_count
    dma = pltpu.SemaphoreType.DMA
    buffer = pltpu.VMEM((tm_count, rows, channels), jnp.bfloat16)
    made, left, last = pl.pallas_call(
        functools.partial(exchange_kernel, tm_count),
        out_shape=[
            pltpu.VMEM((3, bins, 2, channels, channels), jnp.bfloat16),
            pltpu.VMEM((bins, 2 * channels, depth), jnp.bfloat16),
            pltpu.VMEM((bins, depth, channels), jnp.bfloat16),
        ],
        in_specs=[pl.BlockSpec(memory_space=pltpu.HBM)] * 2,
        out_specs=[pl.BlockSpec(memory_space=pltpu.VMEM)] * 3,
        scratch_shapes=[
            pltpu.VMEM((groups, group), jnp.int32),
            pltpu.VMEM((windows, samples, channels), jnp.bfloat16),
            pltpu.VMEM((2, 2 * group, samples), jnp.bfloat16),
            pltpu.VMEM((groups, 2 * group, windows * channels), jnp.float32),
            buffer, buffer, buffer, buffer, buffer,
            pltpu.VMEM((tm_count * rows, channels), jnp.float32),
            pltpu.VMEM((bins, depth, channels), jnp.bfloat16),
            dma((2,)), dma, dma((chips,)),
            dma, dma((chips,)), dma, dma, dma, dma,
        ],
        compiler_params=pltpu.CompilerParams(
            collective_id=0, has_side_effects=True, vmem_limit_bytes=40 << 20),
        name="exchange",
    )(
        pltpu.with_memory_space_constraint(band_bins.reshape(groups, group), pltpu.HBM),
        pltpu.with_memory_space_constraint(traces, pltpu.HBM),
    )

    return pl.pallas_call(
        place_kernel,
        out_shape=jax.ShapeDtypeStruct((1, 4, bins, 2, channels, channels), jnp.bfloat16),
        in_specs=[pl.BlockSpec(memory_space=pltpu.SMEM), pl.BlockSpec(memory_space=pl.ANY)]
        + [pl.BlockSpec(memory_space=pltpu.VMEM)] * 3,
        out_specs=pl.BlockSpec(memory_space=pl.ANY),
        scratch_shapes=[
            pltpu.SMEM((1, 4), jnp.int32),
            pltpu.VMEM((bins, 2, channels, channels), jnp.bfloat16),
            pltpu.VMEM((bins // 4, 2, channels, channels), jnp.bfloat16),
            pltpu.SemaphoreType.DMA,
            pltpu.SemaphoreType.DMA,
        ],
        compiler_params=pltpu.CompilerParams(vmem_limit_bytes=40 << 20),
        name="place",
    )(
        partner_counts,
        pltpu.with_memory_space_constraint(partners, pltpu.HBM),
        made, left, last,
    )


def solution(mesh):
    placed = (P("tm", None, "chan"), P(), P("chan", None), P("chan"))
    return jax.shard_map(
        body,
        mesh=mesh,
        in_specs=placed,
        out_specs=P("chan", None, "tm", None, None, None),
        check_vma=False,
    )
```

time: 120 us -> 40.9 us (0.34)
  the two profiles are of different devices: /device:TPU:352 before, /device:TPU:225 now
where the time goes in v2:
time: 40.9 us; the launch traced here: 40.7 us
  Pallas kernels  40 us (98%)
  between operations  0.66 us (2%)
    pallas_call x1, Pallas kernels, body(): pl.pallas_call(functools.partial(exchange_kernel, tm_count), out_shape=[p...  37.7 us
    pallas_call x1, Pallas kernels, body(): pl.pallas_call(place_kernel, out_shape=jax.ShapeDtypeStruct((1, 4, bins,...  2.33 us

profile of v2, /device:TPU:225, one launch (start us, length us, event | category | flops | bytes accessed | tf_op | source)
XLA Modules:
  0.0 40.7 jit_solution(10664272352073649339)
XLA Ops:
  0.7 37.7 %exchange.1 = (bf16[3,16,2,128,128]{4,3,2,1,0:T(8,128)(2,1)S(1)}, bf16[16,256,128]{2,1,0:T(8,128)(2,1)S(1)}, bf16[16,128,128]{2,1,0:T(8,128)(2,1)S(1)}) custom-call(s32[4,128]{1,0:T(4,128)} %bitcast.1, bf16[2,1920,128]{2,1,0:T(8,128)(2,1)} %traces_hbm.1), custom_call_target="tpu_custom_call" | custom-call | tf_op jit(solution)/shard_map/exchange/pallas_call | solution.py:283
  38.4 2.3 %place.1 = bf16[1,4,16,2,128,128]{5,4,3,2,1,0:T(8,128)(2,1)} custom-call(s32[1]{0:T(128)S(6)} %copy.5.counts_ref, s32[1,4]{1,0:T(1,128)} %partners_hbm.1, bf16[3,16,2,128,128]{4,3,2,1,0:T(8,128)(2,1)S(1)} %get-tuple-element.8.made_ref, bf16[16,256,128]{2,1,0:T(8,128)(2,1)S(1)} %get-tuple-element.9.left_ref, bf16[16,128,128]{2,1,0:T(8,128)(2,1)S(1)} %get-tuple-element.10.last_ref), custom_call_target="tpu_custom_call" | custom-call | tf_op jit(solution)/shard_map/place/pallas_call | solution.py:311

commit v3 on v2

--- a/solution.py
+++ b/solution.py
@@ -28,9 +28,9 @@
     return c, s
 
 
-def exchange_kernel(tm_count, bins_hbm, traces_hbm, made_ref, left_ref, last_ref, bins_ref, traces_ref, table_ref, spectra_ref,
-                    send_ref, held, upper, lower, second, wide, block_ref, load_sem, out_sem, in_sem,
-                    down_send, down_recv, up_send, up_recv, relay_send, relay_recv):
+def exchange_kernel(tm_count, bins_hbm, traces_hbm, partners_hbm, made_ref, left_ref, last_ref, partners_ref, bins_ref, traces_ref, table_ref, spectra_ref,
+                    send_ref, held, upper, lower, second, wide, block_ref, early, early_second, load_sem, out_sem, in_sem,
+                    down_send, down_recv, up_send, up_recv, relay_send, relay_recv, early_send, early_recv, again_send, again_recv):
     me = lax.axis_index("tm")
     block = lax.axis_index("chan")
     blocks = lax.axis_size("chan")
@@ -53,6 +53,8 @@
     load_traces = pltpu.make_async_copy(traces_hbm, traces_ref, load_sem.at[1])
     load_bins.start()
     load_traces.start()
+    load_partners = pltpu.make_async_copy(partners_hbm, partners_ref, load_sem.at[2])
+    load_partners.start()
 
     @pl.loop(1, tm_count)
     def _(r):
@@ -114,9 +116,38 @@
     def pair(ref, f):
         return ref.at[pl.ds(f * 2, 2)]
 
+    plain = rows - rows // windows
+
+    def first_part(ref, f):
+        return ref.at[pl.ds(f * 2, 2), pl.ds(0, plain)]
+
+    def early_down(hop):
+        return pltpu.make_async_remote_copy(
+            src_ref=early if hop else send_ref.at[:, pl.ds(plain, rows - plain)],
+            dst_ref=early_second if hop else early,
+            send_sem=early_send.at[hop], recv_sem=early_recv.at[hop],
+            device_id=(block - 1, me), device_id_type=MESH)
+
+    def spread_again(hop, ref, to_ref):
+        def one(to):
+            pltpu.make_async_remote_copy(
+                src_ref=ref.at[to], dst_ref=to_ref.at[me, pl.ds(plain, rows - plain)],
+                send_sem=again_send.at[hop], recv_sem=again_recv.at[hop],
+                device_id=(block, to), device_id_type=MESH).start()
+
+        one(chip * 2 + 1 - core)
+
+        @pl.loop(1, chips)
+        def _(step):
+            to = chip_at(step, 1)
+            one(to * 2 + core)
+            one(to * 2 + 1 - core)
+
+        to_ref[me, plain:rows, :] = ref[me]
+
     def down(f):
         return pltpu.make_async_remote_copy(
-            src_ref=pair(held, f), dst_ref=pair(upper, f), send_sem=down_send, recv_sem=down_recv.at[f],
+            src_ref=first_part(held, f), dst_ref=first_part(upper, f), send_sem=down_send, recv_sem=down_recv.at[f],
             device_id=(block - 1, me), device_id_type=MESH)
 
     def up(f):
@@ -126,7 +157,7 @@
 
     def relay(f):
         return pltpu.make_async_remote_copy(
-            src_ref=pair(upper, f), dst_ref=pair(second, f), send_sem=relay_send, recv_sem=relay_recv,
+            src_ref=first_part(upper, f), dst_ref=first_part(second, f), send_sem=relay_send, recv_sem=relay_recv,
             device_id=(block - 1, me), device_id_type=MESH)
 
     def forward(f):
@@ -140,6 +171,10 @@
 
     def wait_for(ref, sem):
         pltpu.make_async_copy(ref, ref, sem).wait()
+
+    @pl.when(has_below)
+    def _():
+        early_down(0).start()
 
     spread(chip * 2 + 1 - core)
 
@@ -176,14 +211,13 @@
 
     @pl.when(has_above)
     def _():
-        @pl.loop(0, chips)
-        def _(step):
-            f = chip_at(step, -1)
-            wait_for(pair(upper, 0), down_recv.at[f])
-
-            @pl.when(has_below)
-            def _():
-                relay(f).start()
+        early_down(0).wait_recv()
+
+        @pl.when(has_below)
+        def _():
+            early_down(1).start()
+
+        spread_again(0, early, upper)
 
     regroup(held, block_ref)
 
@@ -197,8 +231,25 @@
 
     @pl.when(has_above)
     def _():
+        @pl.loop(0, chips)
+        def _(step):
+            f = chip_at(step, -1)
+            wait_for(first_part(upper, 0), down_recv.at[f])
+
+            @pl.when(has_below)
+            def _():
+                relay(f).start()
+
+    @pl.when(has_above)
+    def _():
+        wait_for(early.at[pl.ds(0, tm_count - 1)], again_recv.at[0])
         regroup(upper, block_ref)
         products(1)
+
+    @pl.when(block < blocks - 2)
+    def _():
+        early_down(1).wait_recv()
+        spread_again(1, early_second, second)
 
     @pl.when(has_below)
     def _():
@@ -208,36 +259,45 @@
 
     wait_for(held.at[pl.ds(0, tm_count - 1)], out_sem)
 
+    load_partners.wait()
+    last_window = early.at[pl.ds(0, tm_count - 1)]
+
     @pl.when(has_below)
     def _():
-        wait_for(held, down_send)
+        early_down(0).wait_send()
+        wait_for(held.at[:, pl.ds(0, plain)], down_send)
 
     @pl.when(has_above)
     def _():
         wait_for(held, up_send)
+        wait_for(last_window, again_send.at[0])
 
     @pl.when(has_above & has_below)
     def _():
-        wait_for(held, relay_send)
+        early_down(1).wait_send()
+        wait_for(held.at[:, pl.ds(0, plain)], relay_send)
 
     @pl.when(block < blocks - 2)
     def _():
-        wait_for(second, relay_recv)
+        wait_for(last_window, again_send.at[1])
+        wait_for(last_window, again_recv.at[1])
+        wait_for(second.at[:, pl.ds(0, plain)], relay_recv)
         regroup(second, last_ref)
 
 
-def place_kernel(counts_ref, partners_hbm, made_ref, left_ref, last_ref, out_hbm,
-                 partners_ref, product_ref, zero_ref, load_sem, out_sem):
+def place_kernel(counts_ref, partners_ref, made_ref, left_ref, last_ref, out_hbm,
+                 product_ref, zero_ref, out_sem):
     block = lax.axis_index("chan")
     bins, _, channels = last_ref.shape
     slots = out_hbm.shape[1]
-    load_partners = pltpu.make_async_copy(partners_hbm, partners_ref, load_sem)
-    load_partners.start()
     pltpu.make_async_copy(made_ref.at[0], out_hbm.at[0, 0], out_sem).start()
+    slot_number = lax.broadcasted_iota(jnp.int32, partners_ref.shape, 1)
+    offsets = [None]
+    for slot in range(1, slots):
+        offsets.append(jnp.sum(jnp.where(slot_number == slot, partners_ref[...], 0)) - block)
     zero_ref[...] = jnp.zeros_like(zero_ref)
-    load_partners.wait()
     for slot in range(1, slots):
-        offset = partners_ref[0, slot] - block
+        offset = offsets[slot]
         listed = slot < counts_ref[0]
 
         @pl.when(listed & (offset == 1))
@@ -255,7 +315,7 @@
                 pltpu.make_async_copy(zero_ref, to, out_sem).start()
 
     for slot in range(1, slots):
-        @pl.when((slot < counts_ref[0]) & (partners_ref[0, slot] - block == 2))
+        @pl.when((slot < counts_ref[0]) & (offsets[slot] == 2))
         def _():
             for k in range(bins):
                 both = jnp.dot(left_ref[k], last_ref[k], preferred_element_type=jnp.float32)
@@ -280,15 +340,16 @@
     depth = 2 * windows * tm_count
     dma = pltpu.SemaphoreType.DMA
     buffer = pltpu.VMEM((tm_count, rows, channels), jnp.bfloat16)
-    made, left, last = pl.pallas_call(
+    made, left, last, listed = pl.pallas_call(
         functools.partial(exchange_kernel, tm_count),
         out_shape=[
             pltpu.VMEM((3, bins, 2, channels, channels), jnp.bfloat16),
             pltpu.VMEM((bins, 2 * channels, depth), jnp.bfloat16),
             pltpu.VMEM((bins, depth, channels), jnp.bfloat16),
+            pltpu.VMEM(partners.shape, jnp.int32),
         ],
-        in_specs=[pl.BlockSpec(memory_space=pltpu.HBM)] * 2,
-        out_specs=[pl.BlockSpec(memory_space=pltpu.VMEM)] * 3,
+        in_specs=[pl.BlockSpec(memory_space=pltpu.HBM)] * 3,
+        out_specs=[pl.BlockSpec(memory_space=pltpu.VMEM)] * 4,
         scratch_shapes=[
             pltpu.VMEM((groups, group), jnp.int32),
             pltpu.VMEM((windows, samples, channels), jnp.bfloat16),
@@ -297,8 +358,11 @@
             buffer, buffer, buffer, buffer, buffer,
             pltpu.VMEM((tm_count * rows, channels), jnp.float32),
             pltpu.VMEM((bins, depth, channels), jnp.bfloat16),
-            dma((2,)), dma, dma((chips,)),
+            pltpu.VMEM((tm_count, rows // windows, channels), jnp.bfloat16),
+            pltpu.VMEM((tm_count, rows // windows, channels), jnp.bfloat16),
+            dma((3,)), dma, dma((chips,)),
             dma, dma((chips,)), dma, dma, dma, dma,
+            dma((2,)), dma((2,)), dma((2,)), dma((2,)),
         ],
         compiler_params=pltpu.CompilerParams(
             collective_id=0, has_side_effects=True, vmem_limit_bytes=40 << 20),
@@ -306,27 +370,23 @@
     )(
         pltpu.with_memory_space_constraint(band_bins.reshape(groups, group), pltpu.HBM),
         pltpu.with_memory_space_constraint(traces, pltpu.HBM),
+        pltpu.with_memory_space_constraint(partners, pltpu.HBM),
     )
 
     return pl.pallas_call(
         place_kernel,
         out_shape=jax.ShapeDtypeStruct((1, 4, bins, 2, channels, channels), jnp.bfloat16),
-        in_specs=[pl.BlockSpec(memory_space=pltpu.SMEM), pl.BlockSpec(memory_space=pl.ANY)]
-        + [pl.BlockSpec(memory_space=pltpu.VMEM)] * 3,
+        in_specs=[pl.BlockSpec(memory_space=pltpu.SMEM)] + [pl.BlockSpec(memory_space=pltpu.VMEM)] * 4,
         out_specs=pl.BlockSpec(memory_space=pl.ANY),
         scratch_shapes=[
-            pltpu.SMEM((1, 4), jnp.int32),
             pltpu.VMEM((bins, 2, channels, channels), jnp.bfloat16),
             pltpu.VMEM((bins // 4, 2, channels, channels), jnp.bfloat16),
-            pltpu.SemaphoreType.DMA,
             pltpu.SemaphoreType.DMA,
         ],
         compiler_params=pltpu.CompilerParams(vmem_limit_bytes=40 << 20),
         name="place",
     )(
-        partner_counts,
-        pltpu.with_memory_space_constraint(partners, pltpu.HBM),
-        made, left, last,
+        partner_counts, listed, made, left, last,
     )
 
 

time: 40.9 us -> 40.1 us (0.980)
  the two profiles are of different devices: /device:TPU:225 before, /device:TPU:1 now
where the time goes in v3:
time: 40.1 us; the launch traced here: 40 us
  Pallas kernels  39.3 us (98%)
  between operations  0.66 us (2%)
    pallas_call x1, Pallas kernels, body(): pl.pallas_call(functools.partial(exchange_kernel, tm_count), out_shape=[p...  37.3 us
    pallas_call x1, Pallas kernels, body(): pl.pallas_call(place_kernel, out_shape=jax.ShapeDtypeStruct((1, 4, bins,...  2 us

profile of v3, /device:TPU:1, one launch (start us, length us, event | category | flops | bytes accessed | tf_op | source)
XLA Modules:
  0.0 40.0 jit_solution(6601880741159458554)
XLA Ops:
  0.7 37.3 %exchange.1 = (bf16[3,16,2,128,128]{4,3,2,1,0:T(8,128)(2,1)S(1)}, bf16[16,256,128]{2,1,0:T(8,128)(2,1)S(1)}, bf16[16,128,128]{2,1,0:T(8,128)(2,1)S(1)}, s32[1,4]{1,0:T(1,128)S(1)}) custom-call(s32[4,128]{1,0:T(4,128)} %bitcast.1, bf16[2,1920,128]{2,1,0:T(8,128)(2,1)} %traces_hbm.1, s32[1,4]{1,0:T(1,128)} %partners_hbm.1), custom_call_target="tpu_custom_call" | custom-call | tf_op jit(solution)/shard_map/exchange/pallas_call | solution.py:343
  38.0 2.0 %place.1 = bf16[1,4,16,2,128,128]{5,4,3,2,1,0:T(8,128)(2,1)} custom-call(s32[1]{0:T(128)S(6)} %copy.5.counts_ref, s32[1,4]{1,0:T(1,128)S(1)} %get-tuple-element.9.partners_ref, bf16[3,16,2,128,128]{4,3,2,1,0:T(8,128)(2,1)S(1)} %get-tuple-element.10.made_ref, bf16[16,256,128]{2,1,0:T(8,128)(2,1)S(1)} %get-tuple-element.11.left_ref, ...), custom_call_target="tpu_custom_call" | custom-call | tf_op jit(solution)/shard_map/place/pallas_call | solution.py:376

commit v4 on v3

--- a/solution.py
+++ b/solution.py
@@ -71,19 +71,25 @@
     lane = lax.broadcasted_iota(jnp.int32, (group, LANES), 1).astype(jnp.float32)
     load_bins.wait()
     power = jnp.zeros((1, windows * channels), jnp.float32)
+    half = samples // 2
     for g in range(groups):
         row = bins_ref[g : g + 1, :].astype(jnp.float32)
         number = jnp.broadcast_to(row, (group, group)).T
+        sign = 1 - 2 * (number - 2 * jnp.floor(number * 0.5))
         c, s = unit_circle(number * lane, samples)
         step_c, step_s = unit_circle(number * float(LANES), samples)
-        for q in range(samples // LANES):
-            table_ref[g % 2, :group, q * LANES : (q + 1) * LANES] = c.astype(jnp.bfloat16)
-            table_ref[g % 2, group:, q * LANES : (q + 1) * LANES] = (-s).astype(jnp.bfloat16)
+        s, step_s = -s, -step_s
+        for first in range(0, half, LANES):
+            n = min(LANES, half - first)
+            table_ref[g % 2, :group, first : first + n] = c[:, :n].astype(jnp.bfloat16)
+            table_ref[g % 2, group:, first : first + n] = s[:, :n].astype(jnp.bfloat16)
             c, s = c * step_c - s * step_s, s * step_c + c * step_s
         if g == 0:
             load_traces.wait()
-        both = jnp.concatenate([traces_ref[w] for w in range(windows)], axis=1)
-        y = jnp.dot(table_ref[g % 2], both, preferred_element_type=jnp.float32)
+        halves = [traces_ref[w, i * half : (i + 1) * half] for i in range(2) for w in range(windows)]
+        y = jnp.dot(table_ref[g % 2], jnp.concatenate(halves, axis=1), preferred_element_type=jnp.float32)
+        signs = jnp.concatenate([jnp.concatenate([sign] * windows, axis=1)] * 2, axis=0)
+        y = y[:, : windows * channels] + signs * y[:, windows * channels :]
         spectra_ref[g] = y
         power = power + jnp.sum(y * y, axis=0, keepdims=True)
     scale = lax.rsqrt(power * (1.0 / (2 * bin_count)) + 1e-06)
@@ -185,29 +191,45 @@
         spread(to * 2 + 1 - core)
 
     held[me] = send_ref[me]
+    total = tm_count * windows
+
+    def regroup(ref, to_ref, w):
+        some = ref[:, w * 32 : (w + 1) * 32, :].astype(jnp.float32)
+        wide[...] = some.reshape(tm_count * 32, channels)
+        for j in range(16):
+            for p in range(2):
+                lines = wide[pl.ds(j // 8 * 16 + p * 8 + j % 8, tm_count, stride=32), :]
+                at = p * total + w * tm_count
+                to_ref[j, at : at + tm_count, :] = lines.astype(jnp.bfloat16)
+
+    def products(where):
+        @pl.loop(0, 16, step=4)
+        def _(first):
+            for j in range(4):
+                both = jnp.dot(left_ref[first + j], block_ref[first + j], preferred_element_type=jnp.float32)
+                made_ref[where, first + j] = both.astype(jnp.bfloat16).reshape(2, channels, channels)
+
+    def forward_some(first, last):
+        @pl.loop(first, last)
+        def _(step):
+            f = chip_at(step, -1)
+            wait_for(pair(held, 0), in_sem.at[f])
+            forward(f)
+
+    def relay_some(first, last):
+        @pl.loop(first, last)
+        def _(step):
+            f = chip_at(step, -1)
+            wait_for(first_part(upper, 0), down_recv.at[f])
+
+            @pl.when(has_below)
+            def _():
+                relay(f).start()
+
+    middle = chips // 2
     wait_for(held.at[0], in_sem.at[chip])
     forward(chip)
-
-    @pl.loop(1, chips)
-    def _(step):
-        f = chip_at(step, -1)
-        wait_for(pair(held, 0), in_sem.at[f])
-        forward(f)
-
-    total = tm_count * windows
-
-    def regroup(ref, to_ref):
-        wide[...] = ref[...].astype(jnp.float32).reshape(tm_count * rows, channels)
-        for j in range(16):
-            for p in range(2):
-                lines = wide[pl.ds(j // 8 * 16 + p * 8 + j % 8, total, stride=32), :]
-                to_ref[j, p * total : (p + 1) * total, :] = lines.astype(jnp.bfloat16)
-
-    def products(where):
-        @pl.loop(0, 16)
-        def _(j):
-            both = jnp.dot(left_ref[j], block_ref[j], preferred_element_type=jnp.float32)
-            made_ref[where, j] = both.astype(jnp.bfloat16).reshape(2, channels, channels)
+    forward_some(1, middle)
 
     @pl.when(has_above)
     def _():
@@ -217,9 +239,14 @@
         def _():
             early_down(1).start()
 
+    forward_some(middle, chips)
+
+    @pl.when(has_above)
+    def _():
         spread_again(0, early, upper)
 
-    regroup(held, block_ref)
+    for w in range(windows):
+        regroup(held, block_ref, w)
 
     @pl.loop(0, 16)
     def _(j):
@@ -231,37 +258,33 @@
 
     @pl.when(has_above)
     def _():
-        @pl.loop(0, chips)
-        def _(step):
-            f = chip_at(step, -1)
-            wait_for(first_part(upper, 0), down_recv.at[f])
-
-            @pl.when(has_below)
-            def _():
-                relay(f).start()
-
-    @pl.when(has_above)
-    def _():
-        wait_for(early.at[pl.ds(0, tm_count - 1)], again_recv.at[0])
-        regroup(upper, block_ref)
-        products(1)
+        relay_some(0, middle)
 
     @pl.when(block < blocks - 2)
     def _():
         early_down(1).wait_recv()
         spread_again(1, early_second, second)
 
+    last_window = early.at[pl.ds(0, tm_count - 1)]
+
+    @pl.when(has_above)
+    def _():
+        relay_some(middle, chips)
+        wait_for(last_window, again_recv.at[0])
+        for w in range(windows):
+            regroup(upper, block_ref, w)
+        products(1)
+
     @pl.when(has_below)
     def _():
         wait_for(lower, up_recv)
-        regroup(lower, block_ref)
+        for w in range(windows):
+            regroup(lower, block_ref, w)
         products(2)
 
     wait_for(held.at[pl.ds(0, tm_count - 1)], out_sem)
 
     load_partners.wait()
-    last_window = early.at[pl.ds(0, tm_count - 1)]
-
     @pl.when(has_below)
     def _():
         early_down(0).wait_send()
@@ -281,8 +304,10 @@
     def _():
         wait_for(last_window, again_send.at[1])
         wait_for(last_window, again_recv.at[1])
+        for w in range(1, windows):
+            regroup(second, last_ref, w)
         wait_for(second.at[:, pl.ds(0, plain)], relay_recv)
-        regroup(second, last_ref)
+        regroup(second, last_ref, 0)
 
 
 def place_kernel(counts_ref, partners_ref, made_ref, left_ref, last_ref, out_hbm,
@@ -353,10 +378,10 @@
         scratch_shapes=[
             pltpu.VMEM((groups, group), jnp.int32),
             pltpu.VMEM((windows, samples, channels), jnp.bfloat16),
-            pltpu.VMEM((2, 2 * group, samples), jnp.bfloat16),
+            pltpu.VMEM((2, 2 * group, samples // 2), jnp.bfloat16),
             pltpu.VMEM((groups, 2 * group, windows * channels), jnp.float32),
             buffer, buffer, buffer, buffer, buffer,
-            pltpu.VMEM((tm_count * rows, channels), jnp.float32),
+            pltpu.VMEM((tm_count * 32, channels), jnp.float32),
             pltpu.VMEM((bins, depth, channels), jnp.bfloat16),
             pltpu.VMEM((tm_count, rows // windows, channels), jnp.bfloat16),
             pltpu.VMEM((tm_count, rows // windows, channels), jnp.bfloat16),

time: 40.1 us -> 36.7 us (0.915)
  the two profiles are of different devices: /device:TPU:1 before, /device:TPU:225 now
where the time goes in v4:
time: 36.7 us; the launch traced here: 36.5 us
  Pallas kernels  35.9 us (98%)
  between operations  0.66 us (2%)
    pallas_call x1, Pallas kernels, body(): pl.pallas_call(functools.partial(exchange_kernel, tm_count), out_shape=[p...  33.9 us
    pallas_call x1, Pallas kernels, body(): pl.pallas_call(place_kernel, out_shape=jax.ShapeDtypeStruct((1, 4, bins,...  2 us

profile of v4, /device:TPU:225, one launch (start us, length us, event | category | flops | bytes accessed | tf_op | source)
XLA Modules:
  0.0 36.5 jit_solution(13549365228766814554)
XLA Ops:
  0.7 33.9 %exchange.1 = (bf16[3,16,2,128,128]{4,3,2,1,0:T(8,128)(2,1)S(1)}, bf16[16,256,128]{2,1,0:T(8,128)(2,1)S(1)}, bf16[16,128,128]{2,1,0:T(8,128)(2,1)S(1)}, s32[1,4]{1,0:T(1,128)S(1)}) custom-call(s32[4,128]{1,0:T(4,128)} %bitcast.1, bf16[2,1920,128]{2,1,0:T(8,128)(2,1)} %traces_hbm.1, s32[1,4]{1,0:T(1,128)} %partners_hbm.1), custom_call_target="tpu_custom_call" | custom-call | tf_op jit(solution)/shard_map/exchange/pallas_call | solution.py:368
  34.5 2.0 %place.1 = bf16[1,4,16,2,128,128]{5,4,3,2,1,0:T(8,128)(2,1)} custom-call(s32[1]{0:T(128)S(6)} %copy.5.counts_ref, s32[1,4]{1,0:T(1,128)S(1)} %get-tuple-element.9.partners_ref, bf16[3,16,2,128,128]{4,3,2,1,0:T(8,128)(2,1)S(1)} %get-tuple-element.10.made_ref, bf16[16,256,128]{2,1,0:T(8,128)(2,1)S(1)} %get-tuple-element.11.left_ref, ...), custom_call_target="tpu_custom_call" | custom-call | tf_op jit(solution)/shard_map/place/pallas_call | solution.py:401

commit v5 on v4

--- a/solution.py
+++ b/solution.py
@@ -52,21 +52,21 @@
     load_bins = pltpu.make_async_copy(bins_hbm, bins_ref, load_sem.at[0])
     load_traces = pltpu.make_async_copy(traces_hbm, traces_ref, load_sem.at[1])
     load_bins.start()
+    load_partners = pltpu.make_async_copy(partners_hbm, partners_ref, load_sem.at[2])
+
+    @pl.when(has_below)
+    def _():
+        pl.semaphore_signal(barrier, inc=1, device_id=(block - 1, me), device_id_type=MESH)
+
+    @pl.when(has_above)
+    def _():
+        pl.semaphore_signal(barrier, inc=1, device_id=(block + 1, me), device_id_type=MESH)
+
+    for r in range(1, tm_count):
+        pl.semaphore_signal(barrier, inc=1, device_id=(block, lax.rem(me + r, tm_count)), device_id_type=MESH)
+
     load_traces.start()
-    load_partners = pltpu.make_async_copy(partners_hbm, partners_ref, load_sem.at[2])
     load_partners.start()
-
-    @pl.loop(1, tm_count)
-    def _(r):
-        pl.semaphore_signal(barrier, inc=1, device_id=(block, lax.rem(me + r, tm_count)), device_id_type=MESH)
-
-    @pl.when(has_below)
-    def _():
-        pl.semaphore_signal(barrier, inc=1, device_id=(block - 1, me), device_id_type=MESH)
-
-    @pl.when(has_above)
-    def _():
-        pl.semaphore_signal(barrier, inc=1, device_id=(block + 1, me), device_id_type=MESH)
 
     lane = lax.broadcasted_iota(jnp.int32, (group, LANES), 1).astype(jnp.float32)
     load_bins.wait()
@@ -77,8 +77,10 @@
         number = jnp.broadcast_to(row, (group, group)).T
         sign = 1 - 2 * (number - 2 * jnp.floor(number * 0.5))
         c, s = unit_circle(number * lane, samples)
-        step_c, step_s = unit_circle(number * float(LANES), samples)
-        s, step_s = -s, -step_s
+        s = -s
+        half_c = jnp.broadcast_to(c[:, LANES // 2 : LANES // 2 + 1], c.shape)
+        half_s = jnp.broadcast_to(s[:, LANES // 2 : LANES // 2 + 1], s.shape)
+        step_c, step_s = half_c * half_c - half_s * half_s, 2 * half_c * half_s
         for first in range(0, half, LANES):
             n = min(LANES, half - first)
             table_ref[g % 2, :group, first : first + n] = c[:, :n].astype(jnp.bfloat16)
@@ -94,23 +96,27 @@
         power = power + jnp.sum(y * y, axis=0, keepdims=True)
     scale = lax.rsqrt(power * (1.0 / (2 * bin_count)) + 1e-06)
     per = group // 16
-    for g in range(groups):
-        y = (spectra_ref[g] * scale).reshape(2, per, 2, 8, windows * channels)
-        parts = []
-        for w in range(windows):
-            for h in range(2):
-                for p in range(2):
-                    parts.append(y[p, :, h, :, w * channels : (w + 1) * channels])
-        send_ref[g * per : (g + 1) * per] = jnp.concatenate(parts, axis=1).astype(jnp.bfloat16)
+
+    def whiten(w):
+        at = slice(w * channels, (w + 1) * channels)
+        for g in range(groups):
+            y = (spectra_ref[g][:, at] * scale[:, at]).reshape(2, per, 2, 8, channels)
+            parts = [y[p, :, h] for h in range(2) for p in range(2)]
+            send_ref[g * per : (g + 1) * per, w * 32 : (w + 1) * 32, :] = jnp.concatenate(parts, axis=1).astype(jnp.bfloat16)
+
+    for w in range(1, windows):
+        whiten(w)
 
     others = has_below.astype(jnp.int32) + has_above.astype(jnp.int32)
     pl.semaphore_wait(barrier, tm_count - 1 + others)
 
-    def fold(d):
-        return d + d // 2 - 2 * (d // 3)
+    turns = sorted(
+        ((dy, dx) for dy in range(side) for dx in range(side)),
+        key=lambda at: (min(at[0], side - at[0]) + min(at[1], side - at[1]), max(at), at),
+    )
 
     def chip_at(step, sign):
-        dy, dx = fold(step // side), fold(lax.rem(step, side))
+        dy, dx = turns[step]
         return lax.rem(chip_y + sign * dy + side, side) * side + lax.rem(chip_x + sign * dx + side, side)
 
     def spread(to):
@@ -143,8 +149,7 @@
 
         one(chip * 2 + 1 - core)
 
-        @pl.loop(1, chips)
-        def _(step):
+        for step in range(1, chips):
             to = chip_at(step, 1)
             one(to * 2 + core)
             one(to * 2 + 1 - core)
@@ -182,10 +187,10 @@
     def _():
         early_down(0).start()
 
+    whiten(0)
     spread(chip * 2 + 1 - core)
 
-    @pl.loop(1, chips)
-    def _(step):
+    for step in range(1, chips):
         to = chip_at(step, 1)
         spread(to * 2 + core)
         spread(to * 2 + 1 - core)
@@ -210,15 +215,13 @@
                 made_ref[where, first + j] = both.astype(jnp.bfloat16).reshape(2, channels, channels)
 
     def forward_some(first, last):
-        @pl.loop(first, last)
-        def _(step):
+        for step in range(first, last):
             f = chip_at(step, -1)
             wait_for(pair(held, 0), in_sem.at[f])
             forward(f)
 
     def relay_some(first, last):
-        @pl.loop(first, last)
-        def _(step):
+        for step in range(first, last):
             f = chip_at(step, -1)
             wait_for(first_part(upper, 0), down_recv.at[f])
 
@@ -315,7 +318,12 @@
     block = lax.axis_index("chan")
     bins, _, channels = last_ref.shape
     slots = out_hbm.shape[1]
-    pltpu.make_async_copy(made_ref.at[0], out_hbm.at[0, 0], out_sem).start()
+    def put(where, slot):
+        for k in range(0, bins, bins // 4):
+            part = pl.ds(k, bins // 4)
+            pltpu.make_async_copy(made_ref.at[where, part], out_hbm.at[0, slot, part], out_sem).start()
+
+    put(0, 0)
     slot_number = lax.broadcasted_iota(jnp.int32, partners_ref.shape, 1)
     offsets = [None]
     for slot in range(1, slots):
@@ -327,11 +335,11 @@
 
         @pl.when(listed & (offset == 1))
         def _():
-            pltpu.make_async_copy(made_ref.at[1], out_hbm.at[0, slot], out_sem).start()
+            put(1, slot)
 
         @pl.when(listed & (offset == -1))
         def _():
-            pltpu.make_async_copy(made_ref.at[2], out_hbm.at[0, slot], out_sem).start()
+            put(2, slot)
 
         @pl.when(jnp.logical_not(listed))
         def _():

time: 36.7 us -> 36.6 us (level)
  no operation moved by 1% of the time
where the time goes in v5:
time: 36.6 us; the launch traced here: 36.3 us
  Pallas kernels  35.6 us (97%)
  between operations  0.66 us (2%)
    pallas_call x1, Pallas kernels, body(): pl.pallas_call(functools.partial(exchange_kernel, tm_count), out_shape=[p...  33.6 us
    pallas_call x1, Pallas kernels, body(): pl.pallas_call(place_kernel, out_shape=jax.ShapeDtypeStruct((1, 4, bins,...  2 us

profile of v5, /device:TPU:225, one launch (start us, length us, event | category | flops | bytes accessed | tf_op | source)
XLA Modules:
  0.0 36.3 jit_solution(11695701275761541926)
XLA Ops:
  0.7 33.6 %exchange.1 = (bf16[3,16,2,128,128]{4,3,2,1,0:T(8,128)(2,1)S(1)}, bf16[16,256,128]{2,1,0:T(8,128)(2,1)S(1)}, bf16[16,128,128]{2,1,0:T(8,128)(2,1)S(1)}, s32[1,4]{1,0:T(1,128)S(1)}) custom-call(s32[4,128]{1,0:T(4,128)} %bitcast.1, bf16[2,1920,128]{2,1,0:T(8,128)(2,1)} %traces_hbm.1, s32[1,4]{1,0:T(1,128)} %partners_hbm.1), custom_call_target="tpu_custom_call" | custom-call | tf_op jit(solution)/shard_map/exchange/pallas_call | solution.py:376
  34.3 2.0 %place.1 = bf16[1,4,16,2,128,128]{5,4,3,2,1,0:T(8,128)(2,1)} custom-call(s32[1]{0:T(128)S(6)} %copy.5.counts_ref, s32[1,4]{1,0:T(1,128)S(1)} %get-tuple-element.9.partners_ref, bf16[3,16,2,128,128]{4,3,2,1,0:T(8,128)(2,1)S(1)} %get-tuple-element.10.made_ref, bf16[16,256,128]{2,1,0:T(8,128)(2,1)S(1)} %get-tuple-element.11.left_ref, ...), custom_call_target="tpu_custom_call" | custom-call | tf_op jit(solution)/shard_map/place/pallas_call | solution.py:409
